TPU v7x, 32 devices: a whole 2x2x4 slice. The times are simulated.
32 devices in a mesh: rep: 2 (over y), dec: 4 (over z), tp: 4 (over x, core).
Axes of the slice: x: 2, y: 2, z: 4, core: 2. Of those that a mesh axis runs over, the one named last changes fastest.
Arguments:
- token_states: bfloat16 [64, 2, 5120], P(('rep', 'dec')), parts along dimension 0, may hold values from -6 to 6
- query_rows: bfloat16 [64, 2, 4096], P(('rep', 'dec'), None, 'tp'), parts along dimension 0, may hold values from -400 to 400
- key_weight: bfloat16 [5120, 512], P(None, 'tp'), may hold values from -0.078125 to 0.078125
- value_weight: bfloat16 [5120, 512], P(None, 'tp'), may hold values from -0.078125 to 0.078125
- out_weight: bfloat16 [4096, 2560], P('tp'), may hold values from -0.5 to 0.5
- key_pool: bfloat16 [256, 4, 128, 128], P(('rep', 'dec'), 'tp'), parts along dimension 0, may hold values from -6 to 6
- value_pool: bfloat16 [256, 4, 128, 128], P(('rep', 'dec'), 'tp'), parts along dimension 0, may hold values from -6 to 6
- cached_len: int32 [8, 8], P('rep'), parts along dimension 0, may hold values from 0 to 510, as said below
- page_table: int32 [8, 8, 4], P(('rep', 'dec')), parts along dimension 0, may hold values from 0 to 31, as said below
- migrations: int32 [8, 4], P('rep'), parts along dimension 0, may hold values from 0 to 7, as said below
Outputs:
- mixed: bfloat16 [64, 2, 2560], P(('rep', 'dec')), parts along dimension 0
- key_pool_out: bfloat16 [256, 4, 128, 128], P(('rep', 'dec'), 'tp'), parts along dimension 0
- value_pool_out: bfloat16 [256, 4, 128, 128], P(('rep', 'dec'), 'tp'), parts along dimension 0
There are 2 independent parts, one for each index of `rep`. A program takes and returns all parts, laid end to end along the dimension named above; an argument that names none is the same for every part. Nothing has to cross between parts.
Inputs may be any that keep to these rules, and one draw needn't show every extreme that they name: `migrations`: the groups form pairs g and g + 2; in each pair one group sends and the other receives. The sender of pair i sends one response from each of 2 distinct slots, to the receivers of pairs i and i + 1 (mod 2); every receiver gets 2 responses into distinct slots. Rows are in any order. `cached_len`: 0 exactly for the slots that receive a response; sending groups' slots hold 255 or more tokens, receiving groups' other slots 128 or fewer; in every draw at least one moving response has exactly 510 tokens. `page_table`: each group's table names every page 0 to 31 of its pool once.
All inputs are finite; a program needn't handle non-finite values.
Results may differ from a plain program's by a relative error of at most 0.0059.
Values may be sent and summed in bfloat16 or wider, within the bound.
No kernel may reach another device: no remote copies, remote signals or barrier semaphores. Data moves between devices by JAX's collectives and lax.ppermute only.
A program may use at most 64 MiB of HBM per device.

v0:
```python
import jax
import jax.numpy as jnp
from jax import lax
from jax.sharding import PartitionSpec as P

MIG = 2


def passed_along(x, axis, by):
    count = lax.axis_size(axis)
    return lax.ppermute(x, axis, [(i, (i + by) % count) for i in range(count)])


def send_one(payload, distance):
    return passed_along((payload[0], payload[1], payload[2], payload[3]), "dec", distance)


def local(
    token_states,
    query_rows,
    key_weight,
    value_weight,
    out_weight,
    key_pool,
    value_pool,
    cached_len,
    page_table,
    migrations,
):
    group_index = lax.axis_index("dec")
    group_count = lax.axis_size("dec")
    slot_count = token_states.shape[0]
    pool_pages, kv_heads, page_len, head_dim = key_pool.shape
    local_table = page_table[0]
    pages = local_table.shape[1]
    source_group = migrations[:, 0]
    source_slot = migrations[:, 1]
    target_group = migrations[:, 2]
    target_slot = migrations[:, 3]
    slot_ids = jnp.arange(slot_count, dtype=jnp.int32)
    incoming = (target_group == group_index)[:, None] & (target_slot[:, None] == slot_ids[None, :])
    received = jnp.any(incoming, 0)
    from_group = jnp.sum(jnp.where(incoming, source_group[:, None], 0), 0)
    from_slot = jnp.sum(jnp.where(incoming, source_slot[:, None], 0), 0)
    sent = jnp.any(
        (source_group == group_index)[:, None] & (source_slot[:, None] == slot_ids[None, :]), 0
    )
    own_len = cached_len[group_index]
    length = jnp.where(received, cached_len[from_group, from_slot], own_len)
    live = received | (own_len > 0) & ~sent
    half_count = group_count // 2
    distances = [half_count] + [1] + [1 + half_count]
    gap_out = (target_group - group_index) % group_count
    arrivals = []
    for distance in distances:
        mine = (source_group == group_index) & (gap_out == distance)
        out_slot = jnp.sum(jnp.where(mine, source_slot, 0))
        out_pages = local_table[out_slot]
        arrivals.append(
            send_one(
                (
                    key_pool[out_pages],
                    value_pool[out_pages],
                    token_states[out_slot],
                    query_rows[out_slot],
                ),
                distance,
            )
        )
    arrived = tuple((jnp.stack([item[k] for item in arrivals], 0) for k in range(4)))
    gap_in = (group_index - from_group) % group_count
    picked = jnp.zeros_like(gap_in)
    for number, distance in enumerate(distances):
        picked = jnp.where(gap_in == distance, number, picked)
    arrived_k, arrived_v, arrived_x, arrived_q = arrived
    states = jnp.where(received[:, None, None], arrived_x[picked], token_states)
    query = jnp.where(received[:, None, None], arrived_q[picked], query_rows)
    recv_rank = jnp.cumsum(received.astype(jnp.int32)) - 1
    ranks = jnp.arange(MIG, dtype=jnp.int32)
    selected = received[None, :] & (recv_rank[None, :] == ranks[:, None])
    recv_slot = jnp.sum(jnp.where(selected, slot_ids[None, :], 0), 1)
    recv_valid = jnp.any(selected, 1)
    positions = (
        jnp.arange(pages, dtype=jnp.int32)[:, None] * page_len
        + jnp.arange(page_len, dtype=jnp.int32)[None, :]
    )
    keep_in = (positions[None] < length[recv_slot][:, None, None])[:, :, None, :, None]
    zero = jnp.zeros((), key_pool.dtype)
    in_k = jnp.where(keep_in, arrived_k[picked[recv_slot]], zero).reshape(
        -1, kv_heads, page_len, head_dim
    )
    in_v = jnp.where(keep_in, arrived_v[picked[recv_slot]], zero).reshape(
        -1, kv_heads, page_len, head_dim
    )
    dest_pages = jnp.where(recv_valid[:, None], local_table[recv_slot], pool_pages).reshape(-1)
    pool_k = key_pool.at[dest_pages].set(in_k, mode="drop")
    pool_v = value_pool.at[dest_pages].set(in_v, mode="drop")
    step_count = states.shape[1]
    flat = states.reshape(slot_count * step_count, -1)
    new_k = (
        jnp.dot(flat, key_weight, preferred_element_type=jnp.float32)
        .astype(jnp.bfloat16)
        .reshape(slot_count, step_count, kv_heads, head_dim)
    )
    new_v = (
        jnp.dot(flat, value_weight, preferred_element_type=jnp.float32)
        .astype(jnp.bfloat16)
        .reshape(slot_count, step_count, kv_heads, head_dim)
    )
    query = query.reshape(slot_count, step_count, kv_heads, -1, head_dim)
    scaling = head_dim ** (-0.5)
    entry_ids = jnp.arange(slot_count * pages, dtype=jnp.int32)
    owns = local_table.reshape(-1)[None, :] == jnp.arange(pool_pages, dtype=jnp.int32)[:, None]
    page_slot = jnp.sum(jnp.where(owns, entry_ids[None, :] // pages, 0), 1)
    page_index = jnp.sum(jnp.where(owns, entry_ids[None, :] % pages, 0), 1)
    member = page_slot[None, :] == slot_ids[:, None]
    member_f = member.astype(jnp.float32)
    page_query = query[page_slot]
    offsets = jnp.arange(page_len, dtype=jnp.int32)
    inside = page_index[:, None] * page_len + offsets[None, :] < length[page_slot][:, None]
    cached = (
        jnp.einsum("pskgd,pkod->pskgo", page_query, pool_k, preferred_element_type=jnp.float32)
        * scaling
    )
    cached = jnp.where(inside[:, None, None, None, :], cached, -jnp.inf)
    fresh = (
        jnp.einsum("nskgd,ntkd->nskgt", query, new_k, preferred_element_type=jnp.float32) * scaling
    )
    causal = jnp.arange(step_count)[None, :] <= jnp.arange(step_count)[:, None]
    fresh = jnp.where(causal[None, :, None, None, :], fresh, -jnp.inf)
    page_peak = jnp.max(cached, -1)
    slot_peak = jnp.max(jnp.where(member[:, :, None, None, None], page_peak[None], -jnp.inf), 1)
    peak = jnp.maximum(slot_peak, jnp.max(fresh, -1))
    cached_exp = jnp.exp(cached - peak[page_slot][..., None])
    fresh_exp = jnp.exp(fresh - peak[..., None])
    total = jnp.einsum(
        "np,pskg->nskg", member_f, jnp.sum(cached_exp, -1), precision=lax.Precision.HIGHEST
    ) + jnp.sum(fresh_exp, -1)
    cached_w = (cached_exp / total[page_slot][..., None]).astype(jnp.bfloat16)
    fresh_w = (fresh_exp / total[..., None]).astype(jnp.bfloat16)
    page_out = jnp.einsum("pskgo,pkod->pskgd", cached_w, pool_v, preferred_element_type=jnp.float32)
    out = jnp.einsum("np,pskgd->nskgd", member_f, page_out, precision=lax.Precision.HIGHEST)
    out = out + jnp.einsum("nskgt,ntkd->nskgd", fresh_w, new_v, preferred_element_type=jnp.float32)
    attention = out.astype(jnp.bfloat16).reshape(slot_count * step_count, -1)
    partial_value = jnp.dot(attention, out_weight, preferred_element_type=jnp.float32)
    partial_value = jnp.where(
        live[:, None, None], partial_value.reshape(slot_count, step_count, -1), 0.0
    )
    mixed = lax.psum(partial_value, "tp").astype(jnp.bfloat16)
    token_pos = length[:, None] + jnp.arange(step_count, dtype=jnp.int32)[None, :]
    token_page = jnp.take_along_axis(local_table, token_pos // page_len, 1)
    token_page = jnp.where(live[:, None], token_page, pool_pages).reshape(-1)
    token_off = (token_pos % page_len).reshape(-1)
    key_out = pool_k.at[token_page, :, token_off].set(
        new_k.reshape(-1, kv_heads, head_dim), mode="drop"
    )
    value_out = pool_v.at[token_page, :, token_off].set(
        new_v.reshape(-1, kv_heads, head_dim), mode="drop"
    )
    return (mixed, key_out, value_out)


def solution(mesh):
    placed = (
        P(("rep", "dec"), None, None),
        P(("rep", "dec"), None, "tp"),
        P(None, "tp"),
        P(None, "tp"),
        P("tp", None),
        P(("rep", "dec"), "tp", None, None),
        P(("rep", "dec"), "tp", None, None),
        P("rep", None),
        P(("rep", "dec"), None, None),
        P("rep", None),
    )
    return jax.shard_map(
        local,
        mesh=mesh,
        in_specs=placed,
        out_specs=(
            P(("rep", "dec"), None, None),
            P(("rep", "dec"), "tp", None, None),
            P(("rep", "dec"), "tp", None, None),
        ),
        check_vma=False,
    )
```

profile of v0, /device:TPU:0, one launch (start us, length us, event | category | flops | bytes accessed | tf_op | source)
XLA Modules:
  0.0 102.3 jit_solution(3999367189181447767)
XLA Ops:
  0.7 1.4 %copy.74 = bf16[32,1,128,128]{3,2,1,0:T(8,128)(2,1)S(1)} copy(bf16[32,1,128,128]{3,2,1,0:T(8,128)(2,1)} %param.15) | data formatting | bytes 2097152
  3.2 0.7 fusion.62
  9.9 1.2 %gather_fusion.11 = bf16[4,128,128]{2,1,0:T(8,128)(2,1)} fusion(bf16[32,128,128]{2,1,0:T(8,128)(2,1)S(1)} %bitcast.197, s32[1024]{0:T(1024)S(1)} %pad_clamp_fusion.3), kind=kCustom, calls=%fused_computation.11 | custom fusion | bytes 262160 | tf_op jit(solution)/shard_map/gather | solution.py:62
  11.2 5.0 %collective-permute-start.5 = (bf16[4,1,128,128]{3,2,0,1:T(8,128)(2,1)}, bf16[4,1,128,128]{3,2,0,1:T(8,128)(2,1)}, u32[]{:S(2)}, u32[]{:S(2)}) collective-permute-start(bf16[4,1,128,128]{3,2,0,1:T(8,128)(2,1)} %bitcast.37), channel_id=1, source_target_pairs={{0,12},{4,0},{8,4},{12,8},{1,13},{5,1},{9,5},{13,9},{2,14},{6,2},{... | collective-permute-start | bytes 393224 | tf_op jit(solution)/shard_map/ppermute | solution.py:11
  16.2 1.2 %gather_fusion.10 = bf16[4,128,128]{2,1,0:T(8,128)(2,1)} fusion(bf16[32,128,128]{2,1,0:T(8,128)(2,1)S(1)} %bitcast.198, s32[1024]{0:T(1024)S(1)} %pad_clamp_fusion.4), kind=kCustom, calls=%fused_computation.10 | custom fusion | bytes 262160 | tf_op jit(solution)/shard_map/gather | solution.py:62
  17.5 3.9 %collective-permute-start.8 = (bf16[2,1024]{1,0:T(2,128)(2,1)S(1)}, bf16[2,1024]{1,0:T(2,128)(2,1)S(1)}, u32[]{:S(2)}, u32[]{:S(2)}) collective-permute-start(bf16[2,1024]{1,0:T(2,128)(2,1)S(1)} %get-tuple-element.39), channel_id=1, source_target_pairs={{0,12},{4,0},{8,4},{12,8},{1,13},{5,1},{9,5},{13,9},{2,14},{6,2},{... | collective-permute-start | bytes 12296 | tf_op jit(solution)/shard_map/ppermute | solution.py:11
  21.3 0.6 collective-permute-start.6
  25.1 0.7 gather_fusion.1
  25.8 0.6 gather_fusion.2
  26.5 0.6 gather_fusion.6
  27.4 0.7 gather_fusion.8
  28.1 1.4 %dynamic-slice_bitcast_fusion.2 = (bf16[2,5120]{1,0:T(2,128)(2,1)}, bf16[2,5120]{1,0:T(2,128)(2,1)}, bf16[2,5120]{1,0:T(2,128)(2,1)}) fusion(bf16[8,2,5120]{2,1,0:T(2,128)(2,1)} %param.10, s32[]{:T(128)S(6)} %select_n.429, s32[]{:T(128)S(6)} %select_n.432, s32[]{:T(128)S(6)} %select_n.435), kind=kLoop, calls=%fused_computation.60 | loop fusion | bytes 122892 | tf_op jit(solution)/shard_map/squeeze | solution.py:64
  30.0 0.7 gather_fusion.18
  30.8 0.7 broadcast_compare_fusion
  32.1 1.2 %gather_fusion.5 = bf16[4,128,128]{2,1,0:T(8,128)(2,1)} fusion(bf16[32,128,128]{2,1,0:T(8,128)(2,1)S(1)} %bitcast.202, s32[1024]{0:T(1024)S(1)} %pad_clamp_fusion.3), kind=kCustom, calls=%fused_computation.5 | custom fusion | bytes 262160 | tf_op jit(solution)/shard_map/gather | solution.py:63
  33.3 1.2 %gather_fusion.4 = bf16[4,128,128]{2,1,0:T(8,128)(2,1)} fusion(bf16[32,128,128]{2,1,0:T(8,128)(2,1)S(1)} %bitcast.203, s32[1024]{0:T(1024)S(1)} %pad_clamp_fusion.4), kind=kCustom, calls=%fused_computation.4 | custom fusion | bytes 262160 | tf_op jit(solution)/shard_map/gather | solution.py:63
  34.5 1.2 %gather_fusion.9 = bf16[4,128,128]{2,1,0:T(8,128)(2,1)} fusion(bf16[32,128,128]{2,1,0:T(8,128)(2,1)S(1)} %bitcast.199, s32[1024]{0:T(1024)S(1)} %pad_clamp_fusion.5), kind=kCustom, calls=%fused_computation.9 | custom fusion | bytes 262160 | tf_op jit(solution)/shard_map/gather | solution.py:62
  35.7 1.2 %gather_fusion.3 = bf16[4,128,128]{2,1,0:T(8,128)(2,1)} fusion(bf16[32,128,128]{2,1,0:T(8,128)(2,1)S(1)} %bitcast.204, s32[1024]{0:T(1024)S(1)} %pad_clamp_fusion.5), kind=kCustom, calls=%fused_computation.3 | custom fusion | bytes 262160 | tf_op jit(solution)/shard_map/gather | solution.py:63
  37.0 3.3 %collective-permute-start.11 = (bf16[2,5120]{1,0:T(2,128)(2,1)}, bf16[2,5120]{1,0:T(2,128)(2,1)}, u32[]{:S(2)}, u32[]{:S(2)}) collective-permute-start(bf16[2,5120]{1,0:T(2,128)(2,1)} %get-tuple-element.36), channel_id=1, source_target_pairs={{0,12},{4,0},{8,4},{12,8},{1,13},{5,1},{9,5},{13,9},{2,14},{6,2},{... | collective-permute-start | bytes 61448 | tf_op jit(solution)/shard_map/ppermute | solution.py:11
  40.8 1.5 %collective-permute-start.9 = (bf16[2,5120]{1,0:T(2,128)(2,1)}, bf16[2,5120]{1,0:T(2,128)(2,1)}, u32[]{:S(2)}, u32[]{:S(2)}) collective-permute-start(bf16[2,5120]{1,0:T(2,128)(2,1)} %get-tuple-element.34), channel_id=1, source_target_pairs={{0,8},{4,12},{8,0},{12,4},{1,9},{5,13},{9,1},{13,5},{2,10},{6,14},... | collective-permute-start | bytes 61448 | tf_op jit(solution)/shard_map/ppermute | solution.py:11
  42.3 0.6 gather_fusion.13
  43.1 1.2 %gather_fusion.14 = bf16[32,2,8,128]{3,2,1,0:T(8,128)(2,1)} fusion(bf16[8,2,8,128]{3,2,1,0:T(8,128)(2,1)S(1)} %reshape.1010, s32[1024]{0:T(1024)S(1)} %pad_clamp_fusion.1), kind=kCustom, calls=%fused_computation.14 | custom fusion | bytes 262272 | tf_op jit(solution)/shard_map/gather | solution.py:118
  44.3 1.5 %collective-permute-start.3 = (bf16[4,1,128,128]{3,2,0,1:T(8,128)(2,1)}, bf16[4,1,128,128]{3,2,0,1:T(8,128)(2,1)}, u32[]{:S(2)}, u32[]{:S(2)}) collective-permute-start(bf16[4,1,128,128]{3,2,0,1:T(8,128)(2,1)} %bitcast.211), channel_id=1, source_target_pairs={{0,8},{4,12},{8,0},{12,4},{1,9},{5,13},{9,1},{13,5},{2,10},{6,14},... | collective-permute-start | bytes 393224 | tf_op jit(solution)/shard_map/ppermute | solution.py:11
  46.1 2.9 %collective-permute-start.2 = (bf16[4,1,128,128]{3,2,0,1:T(8,128)(2,1)}, bf16[4,1,128,128]{3,2,0,1:T(8,128)(2,1)}, u32[]{:S(2)}, u32[]{:S(2)}) collective-permute-start(bf16[4,1,128,128]{3,2,0,1:T(8,128)(2,1)} %bitcast.210), channel_id=1, source_target_pairs={{0,12},{4,0},{8,4},{12,8},{1,13},{5,1},{9,5},{13,9},{2,14},{6,2},{... | collective-permute-start | bytes 393224 | tf_op jit(solution)/shard_map/ppermute | solution.py:11
  49.0 0.9 pad_maximum_fusion
  49.9 1.7 %gather_fusion.15 = bf16[8,2,5120]{2,1,0:T(2,128)(2,1)} fusion(bf16[3,2,5120]{2,1,0:T(2,128)(2,1)S(1)} %pad_maximum_fusion, s32[1024]{0:T(1024)} %copy-done.10), kind=kCustom, calls=%fused_computation.15 | custom fusion | bytes 327712 | tf_op jit(solution)/shard_map/gather | solution.py:76
  51.6 1.9 %broadcast_select_fusion = bf16[8,2,5120]{2,1,0:T(2,128)(2,1)} fusion(bf16[8,2,5120]{2,1,0:T(2,128)(2,1)} %gather_fusion.15, bf16[8,2,5120]{2,1,0:T(2,128)(2,1)} %param.10, pred[8]{0:T(512)(128)(4,1)S(1)} %fusion.67), kind=kLoop, calls=%fused_computation.45 | loop fusion | flops 81920 | bytes 491528 | tf_op jit(solution)/shard_map/jit(_where)/select_n | solution.py:76
  53.5 1.6 %reshape.876 = bf16[16,5120]{1,0:T(8,128)(2,1)} reshape(bf16[8,2,5120]{2,1,0:T(2,128)(2,1)} %broadcast_select_fusion) | data formatting | bytes 327680 | tf_op jit(solution)/shard_map/reshape | solution.py:99
  55.2 1.3 %convolution_convert_fusion.1 = bf16[16,128]{1,0:T(8,128)(2,1)S(1)} fusion(bf16[16,5120]{1,0:T(8,128)(2,1)} %reshape.876, bf16[5120,128]{1,0:T(8,128)(2,1)S(1)} %copy-done), kind=kOutput, calls=%fused_computation.39 | convolution fusion | flops 20973568 | bytes 1478656 | tf_op jit(solution)/shard_map/dot_general | solution.py:101
  56.9 1.9 %collective-permute-start = (bf16[4,1,128,128]{3,2,0,1:T(8,128)(2,1)}, bf16[4,1,128,128]{3,2,0,1:T(8,128)(2,1)}, u32[]{:S(2)}, u32[]{:S(2)}) collective-permute-start(bf16[4,1,128,128]{3,2,0,1:T(8,128)(2,1)} %bitcast.15), channel_id=1, source_target_pairs={{0,8},{4,12},{8,0},{12,4},{1,9},{5,13},{9,1},{13,5},{2,10},{6,14},... | collective-permute-start | bytes 393224 | tf_op jit(solution)/shard_map/ppermute | solution.py:11
  59.1 1.8 %maximum_bitcast_fusion.1 = bf16[3,4,128,128]{3,2,1,0:T(8,128)(2,1)} fusion(bf16[1,4,1,128,128]{4,3,1,2,0:T(8,128)(2,1)} %bitcast.38, bf16[1,4,1,128,128]{4,3,1,2,0:T(8,128)(2,1)} %bitcast.36, bf16[1,4,1,128,128]{4,3,1,2,0:T(8,128)(2,1)} %bitcast.34), kind=kLoop, calls=%fused_computation.44 | loop fusion | flops 393216 | bytes 786432 | tf_op jit(solution)/shard_map/stack | solution.py:70
  61.0 2.3 %gather_fusion.12 = bf16[2,4,128,128]{3,2,1,0:T(8,128)(2,1)} fusion(bf16[3,4,128,128]{3,2,1,0:T(8,128)(2,1)} %maximum_bitcast_fusion.1, s32[1024]{0:T(1024)S(1)} %pad_clamp_fusion.2), kind=kCustom, calls=%fused_computation.12 | custom fusion | bytes 524296 | tf_op jit(solution)/shard_map/gather | solution.py:89
  63.2 1.3 %collective-permute-done = bf16[4,1,128,128]{3,2,0,1:T(8,128)(2,1)} collective-permute-done((bf16[4,1,128,128]{3,2,0,1:T(8,128)(2,1)}, bf16[4,1,128,128]{3,2,0,1:T(8,128)(2,1)}, u32[]{:S(2)}, u32[]{:S(2)}) %collective-permute-start) | collective-permute-done | bytes 131104 | tf_op jit(solution)/shard_map/ppermute | solution.py:11
  64.6 1.8 %maximum_bitcast_fusion = bf16[3,4,128,128]{3,2,1,0:T(8,128)(2,1)} fusion(bf16[1,4,1,128,128]{4,3,1,2,0:T(8,128)(2,1)} %bitcast.22, bf16[1,4,1,128,128]{4,3,1,2,0:T(8,128)(2,1)} %bitcast.19, bf16[1,4,1,128,128]{4,3,1,2,0:T(8,128)(2,1)} %bitcast.16), kind=kLoop, calls=%fused_computation.43 | loop fusion | flops 393216 | bytes 786432 | tf_op jit(solution)/shard_map/stack | solution.py:70
  66.4 2.3 %gather_fusion.7 = bf16[2,4,128,128]{3,2,1,0:T(8,128)(2,1)} fusion(bf16[3,4,128,128]{3,2,1,0:T(8,128)(2,1)} %maximum_bitcast_fusion, s32[1024]{0:T(1024)S(1)} %pad_clamp_fusion.2), kind=kCustom, calls=%fused_computation.7 | custom fusion | bytes 524296 | tf_op jit(solution)/shard_map/gather | solution.py:92
  68.7 2.0 %bitcast_select_fusion = (bf16[8,1,128,128]{3,2,0,1:T(8,128)(2,1)}, bf16[8,1,128,128]{3,2,0,1:T(8,128)(2,1)}) fusion(bf16[2,4,128,128]{3,2,1,0:T(8,128)(2,1)} %gather_fusion.12, pred[8,128]{1,0:T(8,128)(4,1)S(1)} %copy-done.14, bf16[2,4,128,128]{3,2,1,0:T(8,128)(2,1)} %gather_fusion.7), kind=kLoop, calls=%fused_computation.46 | loop fusion | flops 262144 | bytes 1049600 | tf_op jit(solution)/shard_map/jit(_where)/select_n | solution.py:89
  70.7 1.7 %scatter_fusion = bf16[32,128,128]{2,1,0:T(8,128)(2,1)S(1)} fusion(bf16[32,128,128]{2,1,0:T(8,128)(2,1)S(1)} %bitcast.205, s32[8]{0:T(128)S(1)} %copy-done.13, bf16[8,128,128]{2,1,0:T(8,128)(2,1)} %bitcast.208), kind=kCustom, calls=%fused_computation.19 | custom fusion | bytes 786464 | tf_op jit(solution)/shard_map/scatter | solution.py:97
  72.4 1.7 %scatter_fusion.1 = bf16[32,128,128]{2,1,0:T(8,128)(2,1)S(1)} fusion(bf16[32,128,128]{2,1,0:T(8,128)(2,1)S(1)} %bitcast.200, s32[8]{0:T(128)S(1)} %copy-done.13, bf16[8,128,128]{2,1,0:T(8,128)(2,1)} %bitcast.207), kind=kCustom, calls=%fused_computation.20 | custom fusion | bytes 786464 | tf_op jit(solution)/shard_map/scatter | solution.py:96
  74.1 2.3 %fusion.68 = (f32[32,2,8]{2,1,0:T(2,128)S(1)}, f32[32,2,1,8,128]{4,3,1,0,2:T(8,128)}) fusion(bf16[32,2,8,128]{3,2,1,0:T(8,128)(2,1)} %gather_fusion.14, bf16[32,128,128]{2,1,0:T(8,128)(2,1)S(1)} %scatter_fusion.1, pred[32,128]{1,0:T(8,128)(4,1)S(1)} %add_compare_fusion), kind=kOutput, calls=%fused_computation.205 | convolution fusion | flops 16973312 | bytes 1447936 | tf_op jit(solution)/shard_map/pskgd,pkod->pskgo/dot_general | solution.py:122
  77.2 1.2 %fusion.16 = f32[32,2,8]{2,1,0:T(2,128)S(1)} fusion(f32[32,2,1,8,128]{4,3,1,0,2:T(8,128)} %get-tuple-element.47, f32[32,2,8]{2,1,0:T(2,128)S(1)} %gather_fusion.16), kind=kLoop, calls=%fused_computation.51 | loop fusion | flops 130560 | bytes 266240 | tf_op jit(solution)/shard_map/reduce_sum | solution.py:137
  79.2 0.8 fusion.21
  80.1 1.3 %scatter_fusion.2 = bf16[32,128,128]{2,1,0:T(8,128)(2,1)S(1)} fusion(bf16[32,128,128]{2,1,0:T(8,128)(2,1)S(1)} %scatter_fusion.1, s32[16]{0:T(128)S(1)} %fusion.65, bf16[16,128]{1,0:T(8,128)(2,1)S(1)} %convolution_convert_fusion.1), kind=kCustom, calls=%fused_computation.21 | custom fusion | bytes 12416 | tf_op jit(solution)/shard_map/scatter | solution.py:154
  81.4 2.3 %convolution_bitcast_fusion = f32[32,2,8,128]{3,2,1,0:T(8,128)} fusion(bf16[32,128,128]{2,1,0:T(8,128)(2,1)S(1)} %scatter_fusion, f32[32,2,1,8,128]{4,3,1,0,2:T(8,128)} %get-tuple-element.47, f32[32,2,8]{2,1,0:T(2,128)S(1)} %gather_fusion.17, f32[32,2,8]{2,1,0:T(2,128)S(1)} %gather_fusion.16), kind=kOutput, calls=%fused_computation.26 | convolution fusion | flops 16973824 | bytes 1576960 | tf_op jit(solution)/shard_map/pskgo,pkod->pskgd/dot_general | solution.py:141
  83.7 1.3 %scatter_fusion.3 = bf16[32,128,128]{2,1,0:T(8,128)(2,1)S(1)} fusion(bf16[32,128,128]{2,1,0:T(8,128)(2,1)S(1)} %scatter_fusion, s32[16]{0:T(128)S(1)} %fusion.65, bf16[16,128]{1,0:T(8,128)(2,1)S(1)} %convolution_convert_fusion), kind=kCustom, calls=%fused_computation.22 | custom fusion | bytes 12416 | tf_op jit(solution)/shard_map/scatter | solution.py:157
  85.1 1.4 %fusion.10 = bf16[8,2,1024]{2,0,1:T(8,128)(2,1)S(1)} fusion(f32[32,2,8,128]{3,2,1,0:T(8,128)} %convolution_bitcast_fusion, f32[8,128,2,8]{1,3,2,0:T(8,128)} %fusion.21, s32[32]{0:T(128)S(1)} %copy-done.12), kind=kOutput, calls=%fused_computation.34 | convolution fusion | flops 6324480 | bytes 360576 | tf_op jit(solution)/shard_map/np,pskgd->nskgd/dot_general | solution.py:142
  86.6 3.3 %fusion.2 = f32[8,2,2560]{2,0,1:T(8,128)S(1)} fusion(bf16[8,2,1024]{2,0,1:T(8,128)(2,1)S(1)} %fusion.10, bf16[1024,2560]{1,0:T(8,128)(2,1)} %param.14, pred[8]{0:T(512)(128)(4,1)S(1)} %copy-done.16), kind=kOutput, calls=%fused_computation.25 | convolution fusion | flops 83927040 | bytes 5439496 | tf_op jit(solution)/shard_map/dot_general | solution.py:145
  89.8 11.7 %all-reduce.1 = bf16[8,2,2560]{2,0,1:T(8,128)(2,1)S(1)} all-reduce(f32[8,2,2560]{2,0,1:T(8,128)S(1)} %fusion.2), channel_id=1, replica_groups=mesh['rep'=2,'dec'=4,'tp'=4] {'tp'}, use_global_device_ids=true, to_apply=%region_19.20 | all-reduce | flops 40960 | bytes 245760 | tf_op jit(solution)/shard_map/psum | solution.py:149
  101.6 0.7 copy.54
  (122 shorter events, 9.5 us)
Async XLA Ops:
  0.6 54.5 %copy-start = (bf16[5120,128]{1,0:T(8,128)(2,1)S(1)}, bf16[5120,128]{1,0:T(8,128)(2,1)}, u32[]{:S(2)}) copy-start(bf16[5120,128]{1,0:T(8,128)(2,1)} %param.12) | copy-start | bytes 3932164
  0.6 1.6 %copy-start.7 = (bf16[32,1,128,128]{3,2,1,0:T(8,128)(2,1)S(1)}, bf16[32,1,128,128]{3,2,1,0:T(8,128)(2,1)}, u32[]{:S(2)}) copy-start(bf16[32,1,128,128]{3,2,1,0:T(8,128)(2,1)} %param.16) | copy-start | bytes 3145732
  2.3 0.7 copy-start.8
  2.3 7.4 %copy-start.1 = (s32[1,8,4]{1,2,0:T(4,128)S(1)}, s32[1,8,4]{1,2,0:T(4,128)}, u32[]{:S(2)}) copy-start(s32[1,8,4]{1,2,0:T(4,128)} %param.18) | copy-start | bytes 388
  2.3 15.2 %copy-start.9 = (bf16[8,2,1024]{2,1,0:T(2,128)(2,1)S(1)}, bf16[8,2,1024]{2,1,0:T(2,128)(2,1)}, u32[]{:S(2)}) copy-start(bf16[8,2,1024]{2,1,0:T(2,128)(2,1)} %param.11) | copy-start | bytes 98308
  2.3 20.1 %copy-start.2 = (s32[4,8]{1,0:T(4,128)S(1)}, s32[4,8]{1,0:T(4,128)}, u32[]{:S(2)}) copy-start(s32[4,8]{1,0:T(4,128)} %param.17) | copy-start | bytes 388
  11.2 45.8 %collective-permute-start.5 = (bf16[4,1,128,128]{3,2,0,1:T(8,128)(2,1)}, bf16[4,1,128,128]{3,2,0,1:T(8,128)(2,1)}, u32[]{:S(2)}, u32[]{:S(2)}) collective-permute-start(bf16[4,1,128,128]{3,2,0,1:T(8,128)(2,1)} %bitcast.37), channel_id=1, source_target_pairs={{0,12},{4,0},{8,4},{12,8},{1,13},{5,1},{9,5},{13,9},{2,14},{6,2},{... | collective-permute-start | bytes 393224 | tf_op jit(solution)/shard_map/ppermute | solution.py:11
  17.4 41.7 %collective-permute-start.4 = (bf16[4,1,128,128]{3,2,0,1:T(8,128)(2,1)}, bf16[4,1,128,128]{3,2,0,1:T(8,128)(2,1)}, u32[]{:S(2)}, u32[]{:S(2)}) collective-permute-start(bf16[4,1,128,128]{3,2,0,1:T(8,128)(2,1)} %bitcast.35), channel_id=1, source_target_pairs={{0,4},{4,8},{8,12},{12,0},{1,5},{5,9},{9,13},{13,1},{2,6},{6,10},{... | collective-permute-start | bytes 393224 | tf_op jit(solution)/shard_map/ppermute | solution.py:11
  17.5 19.5 %collective-permute-start.8 = (bf16[2,1024]{1,0:T(2,128)(2,1)S(1)}, bf16[2,1024]{1,0:T(2,128)(2,1)S(1)}, u32[]{:S(2)}, u32[]{:S(2)}) collective-permute-start(bf16[2,1024]{1,0:T(2,128)(2,1)S(1)} %get-tuple-element.39), channel_id=1, source_target_pairs={{0,12},{4,0},{8,4},{12,8},{1,13},{5,1},{9,5},{13,9},{2,14},{6,2},{... | collective-permute-start | bytes 12296 | tf_op jit(solution)/shard_map/ppermute | solution.py:11
  21.3 18.9 %collective-permute-start.7 = (bf16[2,1024]{1,0:T(2,128)(2,1)S(1)}, bf16[2,1024]{1,0:T(2,128)(2,1)S(1)}, u32[]{:S(2)}, u32[]{:S(2)}) collective-permute-start(bf16[2,1024]{1,0:T(2,128)(2,1)S(1)} %get-tuple-element.38), channel_id=1, source_target_pairs={{0,4},{4,8},{8,12},{12,0},{1,5},{5,9},{9,13},{13,1},{2,6},{6,10},{... | collective-permute-start | bytes 12296 | tf_op jit(solution)/shard_map/ppermute | solution.py:11
  21.3 19.4 %collective-permute-start.6 = (bf16[2,1024]{1,0:T(2,128)(2,1)S(1)}, bf16[2,1024]{1,0:T(2,128)(2,1)S(1)}, u32[]{:S(2)}, u32[]{:S(2)}) collective-permute-start(bf16[2,1024]{1,0:T(2,128)(2,1)S(1)} %get-tuple-element.37), channel_id=1, source_target_pairs={{0,8},{4,12},{8,0},{12,4},{1,9},{5,13},{9,1},{13,5},{2,10},{6,14},... | collective-permute-start | bytes 12296 | tf_op jit(solution)/shard_map/ppermute | solution.py:11
  22.5 8.3 %copy-start.15 = (pred[8]{0:T(512)(128)(4,1)}, pred[8]{0:T(512)(128)(4,1)S(1)}, u32[]{:S(2)}) copy-start(pred[8]{0:T(512)(128)(4,1)S(1)} %get-tuple-element.42) | copy-start | bytes 28
  23.2 6.8 %copy-start.11 = (s32[32]{0:T(128)}, s32[32]{0:T(128)S(1)}, u32[]{:S(2)}) copy-start(s32[32]{0:T(128)S(1)} %get-tuple-element.33) | copy-start | bytes 388
  27.4 14.9 %copy-start.10 = (s32[1024]{0:T(1024)}, s32[1024]{0:T(1024)S(1)}, u32[]{:S(2)}) copy-start(s32[1024]{0:T(1024)S(1)} %pad_clamp_fusion) | copy-start | bytes 12292
  37.0 7.3 %collective-permute-start.11 = (bf16[2,5120]{1,0:T(2,128)(2,1)}, bf16[2,5120]{1,0:T(2,128)(2,1)}, u32[]{:S(2)}, u32[]{:S(2)}) collective-permute-start(bf16[2,5120]{1,0:T(2,128)(2,1)} %get-tuple-element.36), channel_id=1, source_target_pairs={{0,12},{4,0},{8,4},{12,8},{1,13},{5,1},{9,5},{13,9},{2,14},{6,2},{... | collective-permute-start | bytes 61448 | tf_op jit(solution)/shard_map/ppermute | solution.py:11
  40.2 5.9 %collective-permute-start.10 = (bf16[2,5120]{1,0:T(2,128)(2,1)}, bf16[2,5120]{1,0:T(2,128)(2,1)}, u32[]{:S(2)}, u32[]{:S(2)}) collective-permute-start(bf16[2,5120]{1,0:T(2,128)(2,1)} %get-tuple-element.35), channel_id=1, source_target_pairs={{0,4},{4,8},{8,12},{12,0},{1,5},{5,9},{9,13},{13,1},{2,6},{6,10},{... | collective-permute-start | bytes 61448 | tf_op jit(solution)/shard_map/ppermute | solution.py:11
  40.8 8.3 %collective-permute-start.9 = (bf16[2,5120]{1,0:T(2,128)(2,1)}, bf16[2,5120]{1,0:T(2,128)(2,1)}, u32[]{:S(2)}, u32[]{:S(2)}) collective-permute-start(bf16[2,5120]{1,0:T(2,128)(2,1)} %get-tuple-element.34), channel_id=1, source_target_pairs={{0,8},{4,12},{8,0},{12,4},{1,9},{5,13},{9,1},{13,5},{2,10},{6,14},... | collective-permute-start | bytes 61448 | tf_op jit(solution)/shard_map/ppermute | solution.py:11
  44.3 14.8 %collective-permute-start.3 = (bf16[4,1,128,128]{3,2,0,1:T(8,128)(2,1)}, bf16[4,1,128,128]{3,2,0,1:T(8,128)(2,1)}, u32[]{:S(2)}, u32[]{:S(2)}) collective-permute-start(bf16[4,1,128,128]{3,2,0,1:T(8,128)(2,1)} %bitcast.211), channel_id=1, source_target_pairs={{0,8},{4,12},{8,0},{12,4},{1,9},{5,13},{9,1},{13,5},{2,10},{6,14},... | collective-permute-start | bytes 393224 | tf_op jit(solution)/shard_map/ppermute | solution.py:11
  46.1 17.1 %collective-permute-start.2 = (bf16[4,1,128,128]{3,2,0,1:T(8,128)(2,1)}, bf16[4,1,128,128]{3,2,0,1:T(8,128)(2,1)}, u32[]{:S(2)}, u32[]{:S(2)}) collective-permute-start(bf16[4,1,128,128]{3,2,0,1:T(8,128)(2,1)} %bitcast.210), channel_id=1, source_target_pairs={{0,12},{4,0},{8,4},{12,8},{1,13},{5,1},{9,5},{13,9},{2,14},{6,2},{... | collective-permute-start | bytes 393224 | tf_op jit(solution)/shard_map/ppermute | solution.py:11
  49.0 14.2 %collective-permute-start.1 = (bf16[4,1,128,128]{3,2,0,1:T(8,128)(2,1)}, bf16[4,1,128,128]{3,2,0,1:T(8,128)(2,1)}, u32[]{:S(2)}, u32[]{:S(2)}) collective-permute-start(bf16[4,1,128,128]{3,2,0,1:T(8,128)(2,1)} %bitcast.209), channel_id=1, source_target_pairs={{0,4},{4,8},{8,12},{12,0},{1,5},{5,9},{9,13},{13,1},{2,6},{6,10},{... | collective-permute-start | bytes 393224 | tf_op jit(solution)/shard_map/ppermute | solution.py:11
  55.2 1.3 %copy-start.5 = (bf16[16,5120]{1,0:T(8,128)(2,1)S(1)}, bf16[16,5120]{1,0:T(8,128)(2,1)}, u32[]{:S(2)}) copy-start(bf16[16,5120]{1,0:T(8,128)(2,1)} %reshape.876) | copy-start | bytes 491524
  55.2 1.5 %copy-start.6 = (bf16[5120,128]{1,0:T(8,128)(2,1)S(1)}, bf16[5120,128]{1,0:T(8,128)(2,1)}, u32[]{:S(2)}) copy-start(bf16[5120,128]{1,0:T(8,128)(2,1)} %param.13) | copy-start | bytes 3932164
  55.2 3.7 %copy-start.18 = (pred[2,2]{1,0:T(4,128)(4,1)S(1)}, pred[2,2]{1,0:T(4,128)(4,1)}, u32[]{:S(2)}) copy-start(pred[2,2]{1,0:T(4,128)(4,1)} %iota_compare_fusion.6) | copy-start | bytes 16
  56.9 7.7 %collective-permute-start = (bf16[4,1,128,128]{3,2,0,1:T(8,128)(2,1)}, bf16[4,1,128,128]{3,2,0,1:T(8,128)(2,1)}, u32[]{:S(2)}, u32[]{:S(2)}) collective-permute-start(bf16[4,1,128,128]{3,2,0,1:T(8,128)(2,1)} %bitcast.15), channel_id=1, source_target_pairs={{0,8},{4,12},{8,0},{12,4},{1,9},{5,13},{9,1},{13,5},{2,10},{6,14},... | collective-permute-start | bytes 393224 | tf_op jit(solution)/shard_map/ppermute | solution.py:11
  59.1 9.6 %copy-start.14 = (pred[8,128]{1,0:T(8,128)(4,1)S(1)}, pred[8,128]{1,0:T(8,128)(4,1)}, u32[]{:S(2)}) copy-start(pred[8,128]{1,0:T(8,128)(4,1)} %broadcast_compare_fusion) | copy-start | bytes 3076
  63.2 7.5 %copy-start.13 = (s32[8]{0:T(128)S(1)}, s32[8]{0:T(128)}, u32[]{:S(2)}) copy-start(s32[8]{0:T(128)} %get-tuple-element.52) | copy-start | bytes 100
  72.4 4.1 %copy-start.17 = (pred[8,32]{1,0:T(8,128)(4,1)S(1)}, pred[8,32]{1,0:T(8,128)(4,1)}, u32[]{:S(2)}) copy-start(pred[8,32]{1,0:T(8,128)(4,1)} %iota_compare_fusion.1) | copy-start | bytes 772
  72.4 6.1 %copy-start.12 = (s32[32]{0:T(128)S(1)}, s32[32]{0:T(128)}, u32[]{:S(2)}) copy-start(s32[32]{0:T(128)} %copy-done.11) | copy-start | bytes 388
  81.4 2.3 %copy-start.3 = (bf16[32,128,128]{2,1,0:T(8,128)(2,1)}, bf16[32,128,128]{2,1,0:T(8,128)(2,1)S(1)}, u32[]{:S(2)}) copy-start(bf16[32,128,128]{2,1,0:T(8,128)(2,1)S(1)} %scatter_fusion.2) | copy-start | bytes 3145732
  81.4 5.1 %copy-start.16 = (pred[8]{0:T(512)(128)(4,1)S(1)}, pred[8]{0:T(512)(128)(4,1)}, u32[]{:S(2)}) copy-start(pred[8]{0:T(512)(128)(4,1)} %copy-done.15) | copy-start | bytes 28
  85.1 4.7 %copy-start.4 = (bf16[32,128,128]{2,1,0:T(8,128)(2,1)}, bf16[32,128,128]{2,1,0:T(8,128)(2,1)S(1)}, u32[]{:S(2)}) copy-start(bf16[32,128,128]{2,1,0:T(8,128)(2,1)S(1)} %scatter_fusion.3) | copy-start | bytes 3145732
where the time goes:
time: 103 us; the launch traced here: 102 us
  local copies, waits for them, and re-layouts  34.2 us (33%)
  starting transfers between devices  21.1 us (20%)
  other arithmetic  14.6 us (14%)
  matrix products  12.1 us (12%)
  blocking collectives  11.7 us (11%)
  between operations  6.86 us (7%)
  waiting for transfers between devices  1.77 us (2%)
    ppermute x12, starting transfers between devices, passed_along(): return lax.ppermute(x, axis, [(i, (i + by) % count) for i in range(count)])  21.1 us
    psum x1, blocking collectives, local(): mixed = lax.psum(partial_value, 'tp').astype(jnp.bfloat16)  11.7 us
    another operation x4, other arithmetic, local(): jnp.stack([item[k] for item in arrivals], 0)  4.52 us
    gather x3, local copies, waits for them, and re-layouts, local(): key_pool[out_pages]  3.64 us
    gather x3, local copies, waits for them, and re-layouts, local(): value_pool[out_pages]  3.63 us
    unnamed x42, local copies, waits for them, and re-layouts  3.31 us
    dot_general x1, matrix products, local(): jnp.dot(attention, out_weight, preferred_element_type=jnp.float32)  3.27 us
    dot_general x1, matrix products, local(): jnp.einsum('pskgo,pkod->pskgd', cached_w, pool_v, preferred_element_type=...  2.3 us
  transfers between devices with their start and end apart: 12, of which 2 were waited for; matrix products, arithmetic and copies ran while one was open for 30% of the time, Pallas kernels for 0%

commit v1 on v0

v1 whole, which is shorter than its diff:
```python
import functools

import jax
import jax.numpy as jnp
from jax import lax
from jax.experimental import pallas as pl
from jax.experimental.pallas import tpu as pltpu
from jax.sharding import PartitionSpec as P

F32 = jnp.float32
BF16 = jnp.bfloat16
SMEM = pl.BlockSpec(memory_space=pltpu.SMEM)
HBM = pl.BlockSpec(memory_space=pltpu.HBM)
ANY = pl.BlockSpec(memory_space=pl.ANY)
VMEM = pl.BlockSpec(memory_space=pltpu.VMEM)


def ring(count, by):
    return [(i, (i + by) % count) for i in range(count)]


def outgoing(mig, me, groups):
    half = groups // 2
    near = jnp.int32(-1)
    far = jnp.int32(-1)
    for m in range(mig.shape[0]):
        mine = mig[m, 0] == me
        gap = lax.rem(mig[m, 2] - me + groups, groups)
        near = jnp.where(mine & (gap == half), mig[m, 1], near)
        far = jnp.where(mine & (gap != half), mig[m, 1], far)
    return near, far


def incoming(mig, lens, me, groups):
    half = groups // 2
    near, far = jnp.int32(-1), jnp.int32(-1)
    near_len, far_len, far_gap = jnp.int32(0), jnp.int32(0), jnp.int32(0)
    for m in range(mig.shape[0]):
        mine = mig[m, 2] == me
        gap = lax.rem(me - mig[m, 0] + groups, groups)
        length = lens[mig[m, 0], mig[m, 1]]
        is_near = mine & (gap == half)
        is_far = mine & (gap != half)
        near = jnp.where(is_near, mig[m, 3], near)
        near_len = jnp.where(is_near, length, near_len)
        far = jnp.where(is_far, mig[m, 3], far)
        far_len = jnp.where(is_far, length, far_len)
        far_gap = jnp.where(is_far, gap, far_gap)
    return near, near_len, far, far_len, far_gap


def pack_kernel(groups, mig, table, key_pool, value_pool, near_out, far_out, sems):
    me = lax.axis_index("dec")
    pages = table.shape[1]
    slots = outgoing(mig, me, groups)
    for n, (slot, out) in enumerate(zip(slots, (near_out, far_out))):

        @pl.when(slot >= 0)
        def _():
            for p in range(pages):
                page = table[0, p, slot]
                pltpu.make_async_copy(key_pool.at[page], out.at[p], sems.at[n, 0, p]).start()
                pltpu.make_async_copy(value_pool.at[page], out.at[pages + p], sems.at[n, 1, p]).start()

    for n, (slot, out) in enumerate(zip(slots, (near_out, far_out))):

        @pl.when(slot >= 0)
        def _():
            for p in range(pages):
                page = table[0, p, slot]
                pltpu.make_async_copy(key_pool.at[page], out.at[p], sems.at[n, 0, p]).wait()
                pltpu.make_async_copy(value_pool.at[page], out.at[pages + p], sems.at[n, 1, p]).wait()


def attend_kernel(
    groups,
    mig,
    lens,
    table,
    states,
    query,
    key_weight,
    value_weight,
    out_weight,
    key_pool,
    value_pool,
    key_out,
    value_out,
    partial,
    new_rows,
    wk,
    wv,
    wo,
    kp,
    vp,
    q_scr,
    a_scr,
    n_scr,
    sems,
):
    me = lax.axis_index("dec")
    slot_count, steps, _ = states.shape
    rows = slot_count * steps
    pages = table.shape[1]
    page_len, head_dim = kp.shape[1:]
    heads = query.shape[2] // head_dim
    span = pages * page_len
    loads = [
        pltpu.make_async_copy(src, dst, sems.at[n])
        for n, (src, dst) in enumerate(
            ((key_weight, wk), (value_weight, wv), (key_pool, kp), (value_pool, vp), (out_weight, wo))
        )
    ]
    for load in loads:
        load.start()
    near, far = outgoing(mig, me, groups)

    qf = query[...].astype(F32)
    for s in range(slot_count):
        for h in range(heads):
            q_scr[pl.ds(h * rows + s * steps, steps), :] = qf[s, :, h * head_dim : (h + 1) * head_dim]
    x = jnp.concatenate([states[s].astype(F32) for s in range(slot_count)], 0).astype(BF16)
    loads[0].wait()
    new_k = jnp.dot(x, wk[...], preferred_element_type=F32).astype(BF16)
    loads[1].wait()
    new_v = jnp.dot(x, wv[...], preferred_element_type=F32).astype(BF16)
    new_rows[:, :head_dim] = new_k
    new_rows[:, head_dim:] = new_v
    n_scr[:, :head_dim] = new_k.astype(F32)
    n_scr[:, head_dim:] = new_v.astype(F32)
    loads[2].wait()
    loads[3].wait()

    scaling = head_dim**-0.5
    count = steps * heads
    fresh_col = lax.broadcasted_iota(jnp.int32, (count, rows), 1)
    fresh_step = lax.broadcasted_iota(jnp.int32, (count, rows), 0) // heads
    position = lax.broadcasted_iota(jnp.int32, (count, span), 1)
    nt = (((1,), (1,)), ((), ()))
    for s in range(slot_count):
        length = lens[me, s]
        numbers = [table[0, p, s] for p in range(pages)]
        keys = jnp.concatenate([kp[n] for n in numbers], 0)
        values = jnp.concatenate([vp[n] for n in numbers], 0)
        qs = jnp.concatenate(
            [q_scr[pl.ds(s * steps + t, heads, stride=rows), :] for t in range(steps)], 0
        ).astype(BF16)
        cached = lax.dot_general(qs, keys, nt, preferred_element_type=F32) * scaling
        cached = jnp.where(position < length, cached, -jnp.inf)
        fresh = lax.dot_general(qs, new_k, nt, preferred_element_type=F32) * scaling
        ok = (fresh_col >= s * steps) & (fresh_col <= s * steps + fresh_step)
        fresh = jnp.where(ok, fresh, -jnp.inf)
        peak = jnp.maximum(jnp.max(cached, 1, keepdims=True), jnp.max(fresh, 1, keepdims=True))
        cached = jnp.exp(cached - peak)
        fresh = jnp.exp(fresh - peak)
        total = jnp.sum(cached, 1, keepdims=True) + jnp.sum(fresh, 1, keepdims=True)
        cached_w = (cached / total).astype(BF16)
        fresh_w = (fresh / total).astype(BF16)
        out = jnp.dot(cached_w, values, preferred_element_type=F32)
        out = out + jnp.dot(fresh_w, new_v, preferred_element_type=F32)
        for t in range(steps):
            a_scr[pl.ds(s * steps + t, heads, stride=rows), :] = out[t * heads : (t + 1) * heads]

    tile = 16
    row = lax.broadcasted_iota(jnp.int32, (tile, head_dim), 0)
    for s in range(slot_count):
        length = lens[me, s]

        @pl.when((length > 0) & (s != near) & (s != far))
        def _():
            for t in range(steps):
                at = length + t
                page = table[0, at // page_len, s]
                offset = lax.rem(at, page_len)
                base = pl.multiple_of(offset // tile * tile, tile)
                hot = row == offset - base
                for pool, low in ((kp, 0), (vp, head_dim)):
                    old = pool[page, pl.ds(base, tile), :].astype(F32)
                    fresh_row = n_scr[s * steps + t : s * steps + t + 1, low : low + head_dim]
                    pool[page, pl.ds(base, tile), :] = jnp.where(hot, fresh_row, old).astype(BF16)

    stores = [
        pltpu.make_async_copy(kp, key_out, sems.at[0]),
        pltpu.make_async_copy(vp, value_out, sems.at[1]),
    ]
    for store in stores:
        store.start()
    attention = jnp.concatenate([a_scr[h * rows : (h + 1) * rows, :].astype(BF16) for h in range(heads)], 1)
    loads[4].wait()
    partial[...] = jnp.dot(attention, wo[...], preferred_element_type=F32).astype(BF16)
    for store in stores:
        store.wait()


def finish_rows_kernel(groups, mig, mine, other, new_rows, total, near_out, far_out, scr):
    me = lax.axis_index("dec")
    near, far = outgoing(mig, me, groups)
    width = mine.shape[1]
    both = (mine[...].astype(F32) + other[...].astype(F32)).astype(BF16)
    total[...] = both
    slot_count, steps, _ = scr.shape
    for s in range(slot_count):
        scr[s, :, :width] = both[s * steps : (s + 1) * steps].astype(F32)
        scr[s, :, width:] = new_rows[s * steps : (s + 1) * steps, :].astype(F32)
    for slot, out in ((near, near_out), (far, far_out)):
        out[...] = scr[jnp.maximum(slot, 0)].astype(BF16)


def mixed_kernel(groups, mig, lens, total, near_in, far_in_a, far_in_b, mixed):
    me = lax.axis_index("dec")
    slot_count, steps, width = mixed.shape
    out_near, out_far = outgoing(mig, me, groups)
    near, _, far, _, far_gap = incoming(mig, lens, me, groups)
    near_rows = near_in[:, :width]
    far_rows = jnp.where(far_gap == 1, far_in_a[:, :width].astype(F32), far_in_b[:, :width].astype(F32))
    for s in range(slot_count):
        live = (lens[me, s] > 0) & (s != out_near) & (s != out_far)
        own = jnp.where(live, total[s * steps : (s + 1) * steps, :].astype(F32), 0.0)
        got = jnp.where(s == near, near_rows.astype(F32), far_rows)
        mixed[s] = jnp.where((s == near) | (s == far), got, own).astype(BF16)


def place_kernel(
    groups,
    mig,
    lens,
    table,
    near_pages,
    far_pages_a,
    far_pages_b,
    near_rows,
    far_rows_a,
    far_rows_b,
    key_in,
    value_in,
    key_out,
    value_out,
    stage,
    in_sems,
    out_sems,
):
    del key_in, value_in
    me = lax.axis_index("dec")
    pages = table.shape[1]
    page_len, head_dim = stage.shape[2:]
    steps = near_rows.shape[0]
    width = near_rows.shape[1] - 2 * head_dim
    near, near_len, far, far_len, far_gap = incoming(mig, lens, me, groups)
    row = lax.broadcasted_iota(jnp.int32, (page_len, head_dim), 0)

    def load(n, source):
        return pltpu.make_async_copy(source, stage.at[n], in_sems.at[n])

    @pl.when(near >= 0)
    def _():
        load(0, near_pages).start()

    @pl.when((far >= 0) & (far_gap == 1))
    def _():
        load(1, far_pages_a).start()

    @pl.when((far >= 0) & (far_gap != 1))
    def _():
        load(1, far_pages_b).start()

    def store(n, slot, p, which):
        pool = (key_out, value_out)[which]
        return pltpu.make_async_copy(
            stage.at[n, which * pages + p], pool.at[table[0, p, slot]], out_sems.at[n, which, p]
        )

    far_rows = jnp.where(far_gap == 1, far_rows_a[:, width:].astype(F32), far_rows_b[:, width:].astype(F32))
    cases = (
        (near, near_len, near_pages, near_rows[:, width:].astype(F32)),
        (far, far_len, far_pages_a, far_rows),
    )
    for n, (slot, length, source, fresh) in enumerate(cases):

        @pl.when(slot >= 0)
        def _():
            load(n, source).wait()
            for p in range(pages):
                at = row + p * page_len
                for which in range(2):
                    page = stage[n, which * pages + p].astype(F32)
                    page = jnp.where(at < length, page, 0.0)
                    for t in range(steps):
                        line = fresh[t : t + 1, which * head_dim : (which + 1) * head_dim]
                        page = jnp.where(at == length + t, line, page)
                    stage[n, which * pages + p] = page.astype(BF16)
                    store(n, slot, p, which).start()

    for n, (slot, _, _, _) in enumerate(cases):

        @pl.when(slot >= 0)
        def _():
            for p in range(pages):
                for which in range(2):
                    store(n, slot, p, which).wait()


def local(
    token_states,
    query_rows,
    key_weight,
    value_weight,
    out_weight,
    key_pool,
    value_pool,
    cached_len,
    page_table,
    migrations,
):
    groups = lax.axis_size("dec")
    half = groups // 2
    tp = lax.axis_size("tp")
    slot_count, steps, model = token_states.shape
    pool_pages, _, page_len, head_dim = key_pool.shape
    rows = slot_count * steps
    width = out_weight.shape[1]
    heads = query_rows.shape[2] // head_dim
    keys = key_pool.reshape(pool_pages, page_len, head_dim)
    values = value_pool.reshape(pool_pages, page_len, head_dim)
    table = jnp.swapaxes(page_table, 1, 2)
    pages = table.shape[1]
    pool_shape = jax.ShapeDtypeStruct(keys.shape, BF16)
    moved_shape = jax.ShapeDtypeStruct((2 * pages, page_len, head_dim), BF16)
    limit = pltpu.CompilerParams(vmem_limit_bytes=48 * 2**20)

    near, far = pl.pallas_call(
        functools.partial(pack_kernel, groups),
        out_shape=(moved_shape, moved_shape),
        in_specs=[SMEM, SMEM, HBM, HBM],
        out_specs=(HBM, HBM),
        scratch_shapes=[pltpu.SemaphoreType.DMA((2, 2, pages))],
        name="pack",
    )(migrations, table, keys, values)
    near_pages = lax.ppermute(near, "dec", ring(groups, half))
    far_pages_a = lax.ppermute(far, "dec", ring(groups, 1))
    far_pages_b = lax.ppermute(far, "dec", ring(groups, 1 + half))

    key_mid, value_mid, partial, new_rows = pl.pallas_call(
        functools.partial(attend_kernel, groups),
        out_shape=(
            pool_shape,
            pool_shape,
            jax.ShapeDtypeStruct((rows, width), BF16),
            jax.ShapeDtypeStruct((rows, 2 * head_dim), BF16),
        ),
        in_specs=[SMEM, SMEM, SMEM, VMEM, VMEM, HBM, HBM, HBM, HBM, HBM],
        out_specs=(HBM, HBM, VMEM, VMEM),
        scratch_shapes=[
            pltpu.VMEM(key_weight.shape, BF16),
            pltpu.VMEM(value_weight.shape, BF16),
            pltpu.VMEM(out_weight.shape, BF16),
            pltpu.VMEM(keys.shape, BF16),
            pltpu.VMEM(values.shape, BF16),
            pltpu.VMEM((heads * rows, head_dim), F32),
            pltpu.VMEM((heads * rows, head_dim), F32),
            pltpu.VMEM((rows, 2 * head_dim), F32),
            pltpu.SemaphoreType.DMA((5,)),
        ],
        compiler_params=limit,
        cost_estimate=pl.CostEstimate(flops=400_000_000, bytes_accessed=14_000_000, transcendentals=65536),
        name="attend",
    )(
        migrations,
        cached_len,
        table,
        token_states,
        query_rows,
        key_weight,
        value_weight,
        out_weight,
        keys,
        values,
    )

    mine, other = partial, lax.ppermute(partial, "tp", [(i, i ^ 1) for i in range(tp)])
    level = 2
    while level < tp:
        mine = (mine.astype(F32) + other.astype(F32)).astype(BF16)
        other = lax.ppermute(mine, "tp", [(i, i ^ level) for i in range(tp)])
        level *= 2
    row_shape = jax.ShapeDtypeStruct((steps, width + 2 * head_dim), BF16)
    total, near_row, far_row = pl.pallas_call(
        functools.partial(finish_rows_kernel, groups),
        out_shape=(jax.ShapeDtypeStruct((rows, width), BF16), row_shape, row_shape),
        in_specs=[SMEM, VMEM, VMEM, VMEM],
        out_specs=(VMEM, VMEM, VMEM),
        scratch_shapes=[pltpu.VMEM((slot_count, steps, width + 2 * head_dim), F32)],
        name="rows",
    )(migrations, mine, other, new_rows)
    near_rows = lax.ppermute(near_row, "dec", ring(groups, half))
    far_rows_a = lax.ppermute(far_row, "dec", ring(groups, 1))
    far_rows_b = lax.ppermute(far_row, "dec", ring(groups, 1 + half))
    mixed = pl.pallas_call(
        functools.partial(mixed_kernel, groups),
        out_shape=jax.ShapeDtypeStruct((slot_count, steps, width), BF16),
        in_specs=[SMEM, SMEM, VMEM, VMEM, VMEM, VMEM],
        out_specs=VMEM,
        name="mixed",
    )(migrations, cached_len, total, near_rows, far_rows_a, far_rows_b)

    key_out, value_out = pl.pallas_call(
        functools.partial(place_kernel, groups),
        out_shape=(pool_shape, pool_shape),
        in_specs=[SMEM, SMEM, SMEM, ANY, ANY, ANY, VMEM, VMEM, VMEM, HBM, HBM],
        out_specs=(HBM, HBM),
        scratch_shapes=[
            pltpu.VMEM((2, 2 * pages, page_len, head_dim), BF16),
            pltpu.SemaphoreType.DMA((2,)),
            pltpu.SemaphoreType.DMA((2, 2, pages)),
        ],
        input_output_aliases={9: 0, 10: 1},
        name="place",
    )(
        migrations,
        cached_len,
        table,
        near_pages,
        far_pages_a,
        far_pages_b,
        near_rows,
        far_rows_a,
        far_rows_b,
        key_mid,
        value_mid,
    )
    return mixed, key_out.reshape(key_pool.shape), value_out.reshape(value_pool.shape)


def solution(mesh):
    placed = (
        P(("rep", "dec"), None, None),
        P(("rep", "dec"), None, "tp"),
        P(None, "tp"),
        P(None, "tp"),
        P("tp", None),
        P(("rep", "dec"), "tp", None, None),
        P(("rep", "dec"), "tp", None, None),
        P("rep", None),
        P(("rep", "dec"), None, None),
        P("rep", None),
    )
    return jax.shard_map(
        local,
        mesh=mesh,
        in_specs=placed,
        out_specs=(
            P(("rep", "dec"), None, None),
            P(("rep", "dec"), "tp", None, None),
            P(("rep", "dec"), "tp", None, None),
        ),
        check_vma=False,
    )
```

time: 103 us -> 74.7 us (0.73)
  local copies, waits for them, and re-layouts: 34.2 us -> 11.5 us
  waiting for transfers between devices: 1.77 us -> 22.3 us
  other arithmetic: 14.6 us -> 0.02 us
  Pallas kernels: 0 us -> 13.4 us
  matrix products: 12.1 us -> 0 us
  blocking collectives: 11.7 us -> 0 us
  between operations: 6.86 us -> 0.74 us
  starting transfers between devices: 21.1 us -> 27 us
    ppermute x12 -> x8, waiting for transfers between devices: 1.77 us -> 22.3 us  [the longest x1 13.7 us: local(): near_rows = lax.ppermute(near_row, 'dec', ring(groups, half))]
    gather x20 -> x0, local copies, waits for them, and re-layouts: 20.5 us -> none  [the longest x3 3.64 us: local(): key_pool[out_pages]]
    pallas_call x0 -> x5, Pallas kernels: none -> 13.4 us  [the longest x1 6.12 us: local(): pl.pallas_call(functools.partial(attend_kernel, groups), out_shape=(pool_...]
    dot_general x9 -> x0, matrix products: 12.1 us -> none  [the longest x1 3.27 us: local(): jnp.dot(attention, out_weight, preferred_element_type=jnp.float32)]
    psum x1 -> x0, blocking collectives: 11.7 us -> none  [local(): mixed = lax.psum(partial_value, 'tp').astype(jnp.bfloat16)]
    unnamed x42 -> x36, local copies, waits for them, and re-layouts: 3.31 us -> 11.5 us
    scatter x4 -> x0, local copies, waits for them, and re-layouts: 6.06 us -> none  [the longest x1 1.68 us: local(): pool_k = key_pool.at[dest_pages].set(in_k, mode='drop')]
    ppermute x12 -> x8, starting transfers between devices: 21.1 us -> 27 us  [the longest x1 15 us: local(): far_pages_a = lax.ppermute(far, 'dec', ring(groups, 1))]
  transfers between devices with their start and end apart: 12 -> 8, of which waited for: 2 -> 3; matrix products, arithmetic and copies ran while one was open for 30% -> 0% of each run, Pallas kernels for 0% -> 6%
where the time goes in v1:
time: 74.7 us; the launch traced here: 74.9 us
  starting transfers between devices  27 us (36%)
  waiting for transfers between devices  22.3 us (30%)
  Pallas kernels  13.4 us (18%)
  local copies, waits for them, and re-layouts  11.5 us (15%)
    ppermute x1, starting transfers between devices, local(): far_pages_a = lax.ppermute(far, 'dec', ring(groups, 1))  15 us
    ppermute x1, waiting for transfers between devices, local(): near_rows = lax.ppermute(near_row, 'dec', ring(groups, half))  13.7 us
    unnamed x36, local copies, waits for them, and re-layouts  11.5 us
    pallas_call x1, Pallas kernels, local(): pl.pallas_call(functools.partial(attend_kernel, groups), out_shape=(pool_...  6.12 us
    ppermute x1, waiting for transfers between devices, local(): far_rows_a = lax.ppermute(far_row, 'dec', ring(groups, 1))  5.67 us
    ppermute x1, starting transfers between devices, local(): far_pages_b = lax.ppermute(far, 'dec', ring(groups, 1 + half))  4.67 us
    ppermute x1, starting transfers between devices, local(): near_pages = lax.ppermute(near, 'dec', ring(groups, half))  2.97 us
    ppermute x1, waiting for transfers between devices, local(): other = lax.ppermute(mine, 'tp', [(i, i ^ level) for i in range(tp)])  2.95 us
  transfers between devices with their start and end apart: 8, of which 3 were waited for; matrix products, arithmetic and copies ran while one was open for 0% of the time, Pallas kernels for 6%

profile of v1, /device:TPU:0, one launch (start us, length us, event | category | flops | bytes accessed | tf_op | source)
XLA Modules:
  0.0 74.9 jit_solution(2341872205927389129)
XLA Ops:
  0.6 0.0 copy-start
  0.6 1.2 %copy-done = bf16[32,1,128,128]{3,2,1,0:T(8,128)(2,1)S(1)} copy-done((bf16[32,1,128,128]{3,2,1,0:T(8,128)(2,1)S(1)}, bf16[32,1,128,128]{3,2,1,0:T(8,128)(2,1)}, u32[]{:S(2)}) %copy-start) | copy-done | bytes 1048600
  1.9 0.0 copy-start.1
  1.9 1.2 %copy-done.1 = bf16[32,1,128,128]{3,2,1,0:T(8,128)(2,1)S(1)} copy-done((bf16[32,1,128,128]{3,2,1,0:T(8,128)(2,1)S(1)}, bf16[32,1,128,128]{3,2,1,0:T(8,128)(2,1)}, u32[]{:S(2)}) %copy-start.1) | copy-done | bytes 1048600
  3.1 0.0 copy-start.2
  3.1 1.3 %copy-done.2 = bf16[5120,128]{1,0:T(8,128)(2,1)S(1)} copy-done((bf16[5120,128]{1,0:T(8,128)(2,1)S(1)}, bf16[5120,128]{1,0:T(8,128)(2,1)}, u32[]{:S(2)}) %copy-start.2) | copy-done | bytes 1310744
  4.4 0.0 copy-start.3
  4.4 1.3 %copy-done.3 = bf16[5120,128]{1,0:T(8,128)(2,1)S(1)} copy-done((bf16[5120,128]{1,0:T(8,128)(2,1)S(1)}, bf16[5120,128]{1,0:T(8,128)(2,1)}, u32[]{:S(2)}) %copy-start.3) | copy-done | bytes 1310744
  5.7 0.9 %copy-done.4 = bf16[8,2,5120]{2,1,0:T(2,128)(2,1)S(1)} copy-done((bf16[8,2,5120]{2,1,0:T(2,128)(2,1)S(1)}, bf16[8,2,5120]{2,1,0:T(2,128)(2,1)}, u32[]{:S(2)}) %copy-start.4) | copy-done | bytes 163864
  6.6 0.7 copy-done.5
  7.3 0.8 %copy-done.6 = bf16[8,2,1024]{2,1,0:T(2,128)(2,1)S(1)} copy-done((bf16[8,2,1024]{2,1,0:T(2,128)(2,1)S(1)}, bf16[8,2,1024]{2,1,0:T(2,128)(2,1)}, u32[]{:S(2)}) %copy-start.6) | copy-done | bytes 32792
  8.1 0.7 copy-done.7
  8.8 0.7 copy-done.8
  9.4 6.1 %attend.1 = (bf16[32,128,128]{2,1,0:T(8,128)(2,1)}, bf16[32,128,128]{2,1,0:T(8,128)(2,1)}, bf16[16,2560]{1,0:T(8,128)(2,1)S(1)}, bf16[16,256]{1,0:T(8,128)(2,1)S(1)}) custom-call(s32[4,4]{1,0:T(4,128)S(1)} %copy-done.5, s32[4,8]{1,0:T(4,128)S(1)} %copy-done.7, s32[1,4,8]{2,1,0:T(4,128)S(1)} %bitcast.15, bf16[8,2,5120]{2,1,0:T(2,128)(2,1)S(1)} %copy-done.4, ...), custom_call_target="tpu_custom_call" | custom-call | flops 400000000 | bytes 14000000 | tf_op jit(solution)/shard_map/attend/pallas_call | solution.py:342
  15.6 0.0 copy-start.9
  15.6 0.6 copy-done.9
  16.2 0.5 collective-permute-start
  16.6 1.0 %pack.1 = (bf16[8,128,128]{2,1,0:T(8,128)(2,1)}, bf16[8,128,128]{2,1,0:T(8,128)(2,1)}) custom-call(s32[4,4]{1,0:T(4,128)} %mig.9, s32[1,4,8]{2,1,0:T(4,128)} %bitcast.13, bf16[32,128,128]{2,1,0:T(8,128)(2,1)} %bitcast.9, bf16[32,128,128]{2,1,0:T(8,128)(2,1)} %bitcast.11), custom_call_target="tpu_custom_call" | custom-call | tf_op jit(solution)/shard_map/pack/pallas_call | solution.py:330
  17.6 4.7 %collective-permute-start.7 = (bf16[8,128,128]{2,1,0:T(8,128)(2,1)}, bf16[8,128,128]{2,1,0:T(8,128)(2,1)S(1)}, u32[]{:S(2)}, u32[]{:S(2)}) collective-permute-start(bf16[8,128,128]{2,1,0:T(8,128)(2,1)} %get-tuple-element.20), channel_id=1, source_target_pairs={{0,12},{4,0},{8,4},{12,8},{1,13},{5,1},{9,5},{13,9},{2,14},{6,2},{... | collective-permute-start | bytes 786440 | tf_op jit(solution)/shard_map/ppermute | solution.py:340
  22.3 15.0 %collective-permute-start.6 = (bf16[8,128,128]{2,1,0:T(8,128)(2,1)}, bf16[8,128,128]{2,1,0:T(8,128)(2,1)S(1)}, u32[]{:S(2)}, u32[]{:S(2)}) collective-permute-start(bf16[8,128,128]{2,1,0:T(8,128)(2,1)} %get-tuple-element.20), channel_id=1, source_target_pairs={{0,4},{4,8},{8,12},{12,0},{1,5},{5,9},{9,13},{13,1},{2,6},{6,10},{... | collective-permute-start | bytes 786440 | tf_op jit(solution)/shard_map/ppermute | solution.py:339
  37.2 3.0 %collective-permute-start.5 = (bf16[8,128,128]{2,1,0:T(8,128)(2,1)}, bf16[8,128,128]{2,1,0:T(8,128)(2,1)S(1)}, u32[]{:S(2)}, u32[]{:S(2)}) collective-permute-start(bf16[8,128,128]{2,1,0:T(8,128)(2,1)} %get-tuple-element.19), channel_id=1, source_target_pairs={{0,8},{4,12},{8,0},{12,4},{1,9},{5,13},{9,1},{13,5},{2,10},{6,14},... | collective-permute-start | bytes 786440 | tf_op jit(solution)/shard_map/ppermute | solution.py:338
  40.2 0.0 collective-permute-done
  40.2 0.0 copy-start.10
  40.2 1.6 %collective-permute-start.1 = (bf16[16,2560]{1,0:T(8,128)(2,1)S(1)}, bf16[16,2560]{1,0:T(8,128)(2,1)S(1)}, u32[]{:S(2)}, u32[]{:S(2)}) collective-permute-start(bf16[16,2560]{1,0:T(8,128)(2,1)S(1)} %add_convert_fusion.mine), channel_id=1, source_target_pairs={{0,2},{1,3},{2,0},{3,1},{4,6},{5,7},{6,4},{7,5},{8,10},{9,11},{10,... | collective-permute-start | bytes 245768 | tf_op jit(solution)/shard_map/ppermute | solution.py:383
  41.8 2.9 %collective-permute-done.1.other = bf16[16,2560]{1,0:T(8,128)(2,1)S(1)} collective-permute-done((bf16[16,2560]{1,0:T(8,128)(2,1)S(1)}, bf16[16,2560]{1,0:T(8,128)(2,1)S(1)}, u32[]{:S(2)}, u32[]{:S(2)}) %collective-permute-start.1) | collective-permute-done | bytes 81952 | tf_op jit(solution)/shard_map/ppermute | solution.py:383
  44.7 0.0 copy-done.10
  44.7 0.6 copy-done.14
  45.4 1.6 %rows.1 = (bf16[16,2560]{1,0:T(8,128)(2,1)}, bf16[2,2816]{1,0:T(2,128)(2,1)}, bf16[2,2816]{1,0:T(2,128)(2,1)}) custom-call(s32[4,4]{1,0:T(4,128)} %mig.9, bf16[16,2560]{1,0:T(8,128)(2,1)} %copy-done.10, bf16[16,2560]{1,0:T(8,128)(2,1)} %copy-done.14, bf16[16,256]{1,0:T(8,128)(2,1)} %copy-done.9), custom_call_target="tpu_custom_call" | custom-call | tf_op jit(solution)/shard_map/rows/pallas_call | solution.py:386
  47.0 0.0 collective-permute-start.2
  47.0 2.4 %collective-permute-start.4 = (bf16[2,2816]{1,0:T(2,128)(2,1)}, bf16[2,2816]{1,0:T(2,128)(2,1)S(1)}, u32[]{:S(2)}, u32[]{:S(2)}) collective-permute-start(bf16[2,2816]{1,0:T(2,128)(2,1)} %get-tuple-element.18), channel_id=1, source_target_pairs={{0,12},{4,0},{8,4},{12,8},{1,13},{5,1},{9,5},{13,9},{2,14},{6,2},{... | collective-permute-start | bytes 33800 | tf_op jit(solution)/shard_map/ppermute | solution.py:396
  49.4 13.7 %collective-permute-done.2.near_in.near_rows = bf16[2,2816]{1,0:T(2,128)(2,1)S(1)} collective-permute-done((bf16[2,2816]{1,0:T(2,128)(2,1)}, bf16[2,2816]{1,0:T(2,128)(2,1)S(1)}, u32[]{:S(2)}, u32[]{:S(2)}) %collective-permute-start.2) | collective-permute-done | bytes 11296 | tf_op jit(solution)/shard_map/ppermute | solution.py:394
  63.0 0.0 collective-permute-start.3
  63.0 0.0 collective-permute-done.4.far_in_b.far_rows_b
  63.0 0.0 copy-start.16
  63.0 5.7 %collective-permute-done.3.far_in_a.far_rows_a = bf16[2,2816]{1,0:T(2,128)(2,1)S(1)} collective-permute-done((bf16[2,2816]{1,0:T(2,128)(2,1)}, bf16[2,2816]{1,0:T(2,128)(2,1)S(1)}, u32[]{:S(2)}, u32[]{:S(2)}) %collective-permute-start.3) | collective-permute-done | bytes 11296 | tf_op jit(solution)/shard_map/ppermute | solution.py:395
  68.7 0.0 copy-done.15
  68.7 0.0 copy-done.16
  68.7 0.6 copy-done.17
  69.3 1.8 %mixed.1 = bf16[8,2,2560]{2,1,0:T(2,128)(2,1)} custom-call(s32[4,4]{1,0:T(4,128)} %mig.9, s32[4,8]{1,0:T(4,128)} %lens.5, bf16[16,2560]{1,0:T(8,128)(2,1)} %get-tuple-element.16.total, bf16[2,2816]{1,0:T(2,128)(2,1)} %copy-done.15, bf16[2,2816]{1,0:T(2,128)(2,1)} %copy-done.17, bf16[2,2816]{1,0:T(2,128)(2,1)} %copy-done.16), custom_call_target="tpu_custom_call" | custom-call | tf_op jit(solution)/shard_map/mixed/pallas_call | solution.py:397
  71.1 0.0 collective-permute-done.5.near_pages
  71.1 0.0 collective-permute-done.7.far_pages_b
  71.1 0.0 copy-start.11
  71.1 0.0 collective-permute-done.6.far_pages_a
  71.1 0.0 copy-start.12
  71.1 0.7 copy-done.13
  71.8 0.1 copy-done.11
  71.9 0.1 copy-done.12
  72.0 2.9 %place.1 = (bf16[32,128,128]{2,1,0:T(8,128)(2,1)}, bf16[32,128,128]{2,1,0:T(8,128)(2,1)}) custom-call(s32[4,4]{1,0:T(4,128)} %mig.9, s32[4,8]{1,0:T(4,128)} %lens.5, s32[1,4,8]{2,1,0:T(4,128)} %bitcast.14, bf16[8,128,128]{2,1,0:T(8,128)(2,1)} %copy-done.13, bf16[8,128,128]{2,1,0:T(8,128)(2,1)} %copy-done.12, ...), custom_call_target="tpu_custom_call", output_to_operand_aliasing={{0}: (9, {}), {1}: (10, {})} | custom-call | tf_op jit(solution)/shard_map/place/pallas_call | solution.py:405
  (10 shorter events, 0.0 us)
Async XLA Ops:
  0.6 1.2 %copy-start = (bf16[32,1,128,128]{3,2,1,0:T(8,128)(2,1)S(1)}, bf16[32,1,128,128]{3,2,1,0:T(8,128)(2,1)}, u32[]{:S(2)}) copy-start(bf16[32,1,128,128]{3,2,1,0:T(8,128)(2,1)} %param.15) | copy-start | bytes 3145732
  1.9 1.2 %copy-start.1 = (bf16[32,1,128,128]{3,2,1,0:T(8,128)(2,1)S(1)}, bf16[32,1,128,128]{3,2,1,0:T(8,128)(2,1)}, u32[]{:S(2)}) copy-start(bf16[32,1,128,128]{3,2,1,0:T(8,128)(2,1)} %param.16) | copy-start | bytes 3145732
  3.1 1.3 %copy-start.2 = (bf16[5120,128]{1,0:T(8,128)(2,1)S(1)}, bf16[5120,128]{1,0:T(8,128)(2,1)}, u32[]{:S(2)}) copy-start(bf16[5120,128]{1,0:T(8,128)(2,1)} %key_weight.1) | copy-start | bytes 3932164
  4.4 1.3 %copy-start.3 = (bf16[5120,128]{1,0:T(8,128)(2,1)S(1)}, bf16[5120,128]{1,0:T(8,128)(2,1)}, u32[]{:S(2)}) copy-start(bf16[5120,128]{1,0:T(8,128)(2,1)} %value_weight.1) | copy-start | bytes 3932164
  5.7 0.9 %copy-start.4 = (bf16[8,2,5120]{2,1,0:T(2,128)(2,1)S(1)}, bf16[8,2,5120]{2,1,0:T(2,128)(2,1)}, u32[]{:S(2)}) copy-start(bf16[8,2,5120]{2,1,0:T(2,128)(2,1)} %states.1) | copy-start | bytes 491524
  6.6 0.7 copy-start.5
  7.3 0.8 %copy-start.6 = (bf16[8,2,1024]{2,1,0:T(2,128)(2,1)S(1)}, bf16[8,2,1024]{2,1,0:T(2,128)(2,1)}, u32[]{:S(2)}) copy-start(bf16[8,2,1024]{2,1,0:T(2,128)(2,1)} %query.1) | copy-start | bytes 98308
  8.1 0.7 copy-start.7
  8.8 0.7 copy-start.8
  15.6 0.6 copy-start.9
  16.2 24.0 %collective-permute-start = (bf16[16,2560]{1,0:T(8,128)(2,1)S(1)}, bf16[16,2560]{1,0:T(8,128)(2,1)S(1)}, u32[]{:S(2)}, u32[]{:S(2)}) collective-permute-start(bf16[16,2560]{1,0:T(8,128)(2,1)S(1)} %get-tuple-element.14), channel_id=1, source_target_pairs={{0,1},{1,0},{2,3},{3,2},{4,5},{5,4},{6,7},{7,6},{8,9},{9,8},{10,11... | collective-permute-start | bytes 245768 | tf_op jit(solution)/shard_map/ppermute | solution.py:379
  17.6 53.5 %collective-permute-start.7 = (bf16[8,128,128]{2,1,0:T(8,128)(2,1)}, bf16[8,128,128]{2,1,0:T(8,128)(2,1)S(1)}, u32[]{:S(2)}, u32[]{:S(2)}) collective-permute-start(bf16[8,128,128]{2,1,0:T(8,128)(2,1)} %get-tuple-element.20), channel_id=1, source_target_pairs={{0,12},{4,0},{8,4},{12,8},{1,13},{5,1},{9,5},{13,9},{2,14},{6,2},{... | collective-permute-start | bytes 786440 | tf_op jit(solution)/shard_map/ppermute | solution.py:340
  22.3 48.8 %collective-permute-start.6 = (bf16[8,128,128]{2,1,0:T(8,128)(2,1)}, bf16[8,128,128]{2,1,0:T(8,128)(2,1)S(1)}, u32[]{:S(2)}, u32[]{:S(2)}) collective-permute-start(bf16[8,128,128]{2,1,0:T(8,128)(2,1)} %get-tuple-element.20), channel_id=1, source_target_pairs={{0,4},{4,8},{8,12},{12,0},{1,5},{5,9},{9,13},{13,1},{2,6},{6,10},{... | collective-permute-start | bytes 786440 | tf_op jit(solution)/shard_map/ppermute | solution.py:339
  37.2 33.8 %collective-permute-start.5 = (bf16[8,128,128]{2,1,0:T(8,128)(2,1)}, bf16[8,128,128]{2,1,0:T(8,128)(2,1)S(1)}, u32[]{:S(2)}, u32[]{:S(2)}) collective-permute-start(bf16[8,128,128]{2,1,0:T(8,128)(2,1)} %get-tuple-element.19), channel_id=1, source_target_pairs={{0,8},{4,12},{8,0},{12,4},{1,9},{5,13},{9,1},{13,5},{2,10},{6,14},... | collective-permute-start | bytes 786440 | tf_op jit(solution)/shard_map/ppermute | solution.py:338
  40.2 4.5 %copy-start.10 = (bf16[16,2560]{1,0:T(8,128)(2,1)}, bf16[16,2560]{1,0:T(8,128)(2,1)S(1)}, u32[]{:S(2)}) copy-start(bf16[16,2560]{1,0:T(8,128)(2,1)S(1)} %add_convert_fusion.mine) | copy-start | bytes 245764
  40.2 4.5 %collective-permute-start.1 = (bf16[16,2560]{1,0:T(8,128)(2,1)S(1)}, bf16[16,2560]{1,0:T(8,128)(2,1)S(1)}, u32[]{:S(2)}, u32[]{:S(2)}) collective-permute-start(bf16[16,2560]{1,0:T(8,128)(2,1)S(1)} %add_convert_fusion.mine), channel_id=1, source_target_pairs={{0,2},{1,3},{2,0},{3,1},{4,6},{5,7},{6,4},{7,5},{8,10},{9,11},{10,... | collective-permute-start | bytes 245768 | tf_op jit(solution)/shard_map/ppermute | solution.py:383
  44.7 0.6 copy-start.14
  47.0 16.0 %collective-permute-start.2 = (bf16[2,2816]{1,0:T(2,128)(2,1)}, bf16[2,2816]{1,0:T(2,128)(2,1)S(1)}, u32[]{:S(2)}, u32[]{:S(2)}) collective-permute-start(bf16[2,2816]{1,0:T(2,128)(2,1)} %get-tuple-element.17), channel_id=1, source_target_pairs={{0,8},{4,12},{8,0},{12,4},{1,9},{5,13},{9,1},{13,5},{2,10},{6,14},... | collective-permute-start | bytes 33800 | tf_op jit(solution)/shard_map/ppermute | solution.py:394
  47.0 16.0 %collective-permute-start.4 = (bf16[2,2816]{1,0:T(2,128)(2,1)}, bf16[2,2816]{1,0:T(2,128)(2,1)S(1)}, u32[]{:S(2)}, u32[]{:S(2)}) collective-permute-start(bf16[2,2816]{1,0:T(2,128)(2,1)} %get-tuple-element.18), channel_id=1, source_target_pairs={{0,12},{4,0},{8,4},{12,8},{1,13},{5,1},{9,5},{13,9},{2,14},{6,2},{... | collective-permute-start | bytes 33800 | tf_op jit(solution)/shard_map/ppermute | solution.py:396
  63.0 5.7 %copy-start.15 = (bf16[2,2816]{1,0:T(2,128)(2,1)}, bf16[2,2816]{1,0:T(2,128)(2,1)S(1)}, u32[]{:S(2)}) copy-start(bf16[2,2816]{1,0:T(2,128)(2,1)S(1)} %collective-permute-done.2.near_in.near_rows) | copy-start | bytes 33796
  63.0 5.7 %collective-permute-start.3 = (bf16[2,2816]{1,0:T(2,128)(2,1)}, bf16[2,2816]{1,0:T(2,128)(2,1)S(1)}, u32[]{:S(2)}, u32[]{:S(2)}) collective-permute-start(bf16[2,2816]{1,0:T(2,128)(2,1)} %get-tuple-element.18), channel_id=1, source_target_pairs={{0,4},{4,8},{8,12},{12,0},{1,5},{5,9},{9,13},{13,1},{2,6},{6,10},{... | collective-permute-start | bytes 33800 | tf_op jit(solution)/shard_map/ppermute | solution.py:395
  63.0 5.7 %copy-start.16 = (bf16[2,2816]{1,0:T(2,128)(2,1)}, bf16[2,2816]{1,0:T(2,128)(2,1)S(1)}, u32[]{:S(2)}) copy-start(bf16[2,2816]{1,0:T(2,128)(2,1)S(1)} %collective-permute-done.4.far_in_b.far_rows_b) | copy-start | bytes 33796
  68.7 0.6 copy-start.17
  71.1 0.7 copy-start.13
  71.1 0.8 %copy-start.11 = (bf16[8,128,128]{2,1,0:T(8,128)(2,1)}, bf16[8,128,128]{2,1,0:T(8,128)(2,1)S(1)}, u32[]{:S(2)}) copy-start(bf16[8,128,128]{2,1,0:T(8,128)(2,1)S(1)} %collective-permute-done.7.far_pages_b) | copy-start | bytes 786436
  71.1 0.9 %copy-start.12 = (bf16[8,128,128]{2,1,0:T(8,128)(2,1)}, bf16[8,128,128]{2,1,0:T(8,128)(2,1)S(1)}, u32[]{:S(2)}) copy-start(bf16[8,128,128]{2,1,0:T(8,128)(2,1)S(1)} %collective-permute-done.6.far_pages_a) | copy-start | bytes 786436
